TPU v7x, 32 devices: a whole 2x2x4 slice. The times are simulated.
32 devices in a mesh: ctx: 8 (over z, core), head: 4 (over y, x).
Axes of the slice: x: 2, y: 2, z: 4, core: 2. Of those that a mesh axis runs over, the one named last changes fastest.
Arguments:
- queries: bfloat16 [4096, 8192], P('ctx', 'head'), may hold values from -136 to 136
- keys: bfloat16 [4096, 8192], P('ctx', 'head'), may hold values from -6 to 6
- values: bfloat16 [4096, 8192], P('ctx', 'head'), may hold values from -6 to 6
- segment_ids: int32 [4096], P('ctx'), may hold values from 0 to 3, never falling along the last dimension, each value on 1 to 2048 neighbouring positions
Outputs:
- attended: bfloat16 [4096, 8192], P('ctx', 'head')
Inputs may be any that keep to these rules, and one draw needn't show every extreme that they name: `segment_ids`: document numbers never fall along the tokens; every document of 0 to 3 appears, with 1 to 2048 tokens, one with exactly 2048.
All inputs are finite; a program needn't handle non-finite values.
Results may differ from a plain program's by a relative error of at most 0.0049.
Values may be sent and summed in bfloat16 or wider, within the bound.
A program may use at most 64 MiB of HBM per device.

v0:
```python
import jax
import jax.numpy as jnp
from jax import lax
from jax.sharding import PartitionSpec as P

HEADS = 64
DH = 128
BLK = 512


def carried_in(value, axis, join, neutral):
    count, mine = (lax.axis_size(axis), lax.axis_index(axis))
    pieces = jax.tree.map(lambda part: lax.all_gather(part, axis), value)
    running = jax.tree.map(
        lambda part, zero: jnp.full_like(part, 0) + jnp.asarray(zero, part.dtype), value, neutral
    )

    def hop(position, running):
        longer = join(running, jax.tree.map(lambda part: part[position], pieces))
        return jax.tree.map(lambda new, old: jnp.where(position < mine, new, old), longer, running)

    return lax.fori_loop(0, count - 1, hop, running)


def combine_states(earlier, later):
    state_e, last_e = earlier
    state_l, last_l = later
    joined = state_l + jnp.where(last_e == last_l, state_e, jnp.zeros_like(state_e))
    state = jnp.where(last_l < 0, state_e, joined)
    last = jnp.where(last_l < 0, last_e, last_l)
    return (state, last)


def on_device(queries, keys, values, segment_ids):
    rows = queries.shape[0]
    heads = queries.shape[1] // DH
    blocks = rows // BLK
    q_all = queries.reshape(blocks, BLK, heads, DH)
    k_all = keys.reshape(blocks, BLK, heads, DH)
    v_all = values.reshape(blocks, BLK, heads, DH)
    s_all = segment_ids.reshape(blocks, BLK)
    positions = jnp.arange(BLK)
    causal = positions[:, None] >= positions[None, :]

    def local_block(item):
        qb, kb, vb, sb = item
        scores = jnp.einsum("thd,shd->hts", qb, kb, preferred_element_type=jnp.float32)
        mask = causal & (sb[:, None] == sb[None, :])
        probs = jnp.where(mask[None], scores, 0.0).astype(jnp.bfloat16)
        intra = jnp.einsum("hts,shd->thd", probs, vb, preferred_element_type=jnp.float32)
        block_last = sb[-1]
        keep = (sb == block_last)[:, None, None]
        kv_sum = jnp.einsum(
            "thd,the->hde",
            jnp.where(keep, kb, jnp.zeros_like(kb)),
            vb,
            preferred_element_type=jnp.float32,
        )
        return (intra, kv_sum, block_last)

    intra_all, kv_all, last_all = lax.map(local_block, (q_all, k_all, v_all, s_all))
    empty_state = (jnp.zeros((heads, DH, DH), jnp.float32), jnp.int32(-1))

    def fold_local(carry, item):
        return (combine_states(carry, item), None)

    own_state, _ = lax.scan(fold_local, empty_state, (kv_all, last_all))
    prefix = carried_in(own_state, "ctx", combine_states, empty_state)

    def inter_block(carry, item):
        qb, sb, kv_sum, block_last = item
        state, last = carry
        inter = jnp.einsum(
            "thd,hde->the", qb, state.astype(jnp.bfloat16), preferred_element_type=jnp.float32
        )
        inter = jnp.where((sb == last)[:, None, None], inter, 0.0)
        return (combine_states(carry, (kv_sum, block_last)), inter)

    _, inter_all = lax.scan(inter_block, prefix, (q_all, s_all, kv_all, last_all))
    outputs = (intra_all + inter_all).reshape(rows, heads * DH)
    squares = jnp.sum(outputs * outputs, axis=1)
    totals = lax.psum(squares, "head")
    scaled = outputs * lax.rsqrt(totals / (HEADS * DH) + 1e-05)[:, None]
    return scaled.astype(jnp.bfloat16)


def solution(mesh):
    in_specs = (P("ctx", "head"), P("ctx", "head"), P("ctx", "head"), P("ctx"))
    out_specs = P("ctx", "head")
    return jax.shard_map(
        on_device, mesh=mesh, in_specs=in_specs, out_specs=out_specs, check_vma=False
    )
```

profile of v0, /device:TPU:0, one launch (start us, length us, event | category | flops | bytes accessed | tf_op | source)
XLA Modules:
  0.0 163.9 jit_solution(9433695894546559031)
XLA Ops:
  6.5 0.0 copy-start
  6.5 0.0 all-gather.3.cloned.1.call-start
  6.5 1.4 slice.4
  8.0 1.3 broadcast_compare_fusion.1
  9.8 3.9 %copy.18 = bf16[512,2048]{0,1:T(8,128)(2,1)} copy(bf16[512,2048]{1,0:T(8,128)(2,1)} %param.7) | data formatting | bytes 4194304 | tf_op jit(solution)/shard_map/while/body/jit(dynamic_index_in_dim)/squeeze | solution.py:61
  13.7 0.0 copy-start.2
  13.7 0.0 copy-start.1
  13.7 4.0 %fusion.14 = f32[16,128,128]{2,1,0:T(8,128)} fusion(bf16[512,16,128]{0,2,1:T(8,128)(2,1)} %bitcast.52, pred[512]{0:T(512)(128)(4,1)S(1)} %broadcast_compare_fusion.1, pred[]{:T(512)S(6)} %lt.38, bf16[512,2048]{1,0:T(8,128)(2,1)} %param.8), kind=kOutput, calls=%fused_computation.18 | convolution fusion | flops 269746176 | bytes 5243393 | tf_op jit(solution)/shard_map/while/body/eval_jaxpr/thd,the->hde/dot_general | solution.py:53
  17.8 0.0 all-gather.3.cloned.1.call-update
  18.4 0.0 copy-done.2
  18.4 0.6 dynamic-slice.2
  19.0 0.7 dynamic-update-slice
  19.6 10.6 %all-reduce = s32[8]{0:T(128)S(1)} all-reduce(s32[8]{0:T(128)S(1)} %dynamic-update-slice), channel_id=1, replica_groups=mesh['ctx'=8,'head'=4] {'ctx'}, use_global_device_ids=true, to_apply=%add | all-reduce | flops 8 | bytes 64
  30.2 0.0 copy-done.1
  30.3 0.2 fusion.20
  30.5 0.0 copy-done
  30.5 9.3 %fusion = f32[16,512,128]{1,2,0:T(8,128)} fusion(bf16[512,16,128]{0,2,1:T(8,128)(2,1)} %bitcast.53, pred[512,512]{1,0:T(8,128)(4,1)S(1)} %fusion.20, bf16[512,2048]{1,0:T(8,128)(2,1)} %param.8, bf16[512,2048]{1,0:T(8,128)(2,1)S(1)} %copy-done), kind=kOutput, calls=%fused_computation.6 | convolution fusion | flops 2155872256 | bytes 10747904 | tf_op jit(solution)/shard_map/while/body/eval_jaxpr/hts,shd->thd/dot_general | solution.py:50
  39.8 62.9 %all-gather.3.cloned.1.call-done = f32[128,128,128]{2,1,0:T(8,128)} async-done(((f32[16,128,128]{2,1,0:T(8,128)}), f32[128,128,128]{2,1,0:T(8,128)}) %all-gather.3.cloned.1.call-update) | async-done | bytes 8388624 | tf_op jit(solution)/shard_map/all_gather | solution.py:13
  102.7 30.2 %while.10 = (s32[]{:T(128)}, f32[16,128,128]{2,1,0:T(8,128)S(1)}, s32[]{:T(128)}, s32[]{:T(128)}, s32[8]{0:T(128)S(1)}, /*index=5*/f32[8,16,128,128]{3,2,1,0:T(8,128)}, s32[]{:T(128)}, s32[]{:T(128)}) while((s32[]{:T(128)}, f32[16,128,128]{2,1,0:T(8,128)S(1)}, s32[]{:T(128)}, s32[]{:T(128)}, s32[8]{0:T(128)S(1)}, ...), condition=%wide.region_1.2_spmd.clone, body=%wide.region_0.1_spmd.clone.sunk | while | flops 1310728 | bytes 3145895 | solution.py:22
  102.7 0.6 dynamic_slice.44
  104.6 1.8 %select_select_fusion.2 = f32[16,128,128]{2,1,0:T(8,128)S(1)} fusion(f32[16,128,128]{2,1,0:T(8,128)S(1)} %get-tuple-element.264, f32[8,16,128,128]{3,2,1,0:T(8,128)} %get-tuple-element.276, s32[]{:T(128)} %get-tuple-element.263, pred[]{:T(512)S(6)} %compare.3, pred[]{:T(512)S(6)} %eq.67, pred[]{:T(512)S(6)} %lt.45, pred[]{:T(512)S(6)} %lt.46), kind=kLoop, calls=%fused_computation.clone.1 | loop fusion | flops 1310720 | bytes 3145736 | tf_op jit(solution)/shard_map/while/body/eval_jaxpr/jit(_where)/select_n | solution.py:20
  107.0 0.6 dynamic_slice.44
  108.9 1.8 %select_select_fusion.2 = f32[16,128,128]{2,1,0:T(8,128)S(1)} fusion(f32[16,128,128]{2,1,0:T(8,128)S(1)} %get-tuple-element.264, f32[8,16,128,128]{3,2,1,0:T(8,128)} %get-tuple-element.276, s32[]{:T(128)} %get-tuple-element.263, pred[]{:T(512)S(6)} %compare.3, pred[]{:T(512)S(6)} %eq.67, pred[]{:T(512)S(6)} %lt.45, pred[]{:T(512)S(6)} %lt.46), kind=kLoop, calls=%fused_computation.clone.1 | loop fusion | flops 1310720 | bytes 3145736 | tf_op jit(solution)/shard_map/while/body/eval_jaxpr/jit(_where)/select_n | solution.py:20
  111.3 0.6 dynamic_slice.44
  113.2 1.8 %select_select_fusion.2 = f32[16,128,128]{2,1,0:T(8,128)S(1)} fusion(f32[16,128,128]{2,1,0:T(8,128)S(1)} %get-tuple-element.264, f32[8,16,128,128]{3,2,1,0:T(8,128)} %get-tuple-element.276, s32[]{:T(128)} %get-tuple-element.263, pred[]{:T(512)S(6)} %compare.3, pred[]{:T(512)S(6)} %eq.67, pred[]{:T(512)S(6)} %lt.45, pred[]{:T(512)S(6)} %lt.46), kind=kLoop, calls=%fused_computation.clone.1 | loop fusion | flops 1310720 | bytes 3145736 | tf_op jit(solution)/shard_map/while/body/eval_jaxpr/jit(_where)/select_n | solution.py:20
  115.6 0.6 dynamic_slice.44
  117.5 1.8 %select_select_fusion.2 = f32[16,128,128]{2,1,0:T(8,128)S(1)} fusion(f32[16,128,128]{2,1,0:T(8,128)S(1)} %get-tuple-element.264, f32[8,16,128,128]{3,2,1,0:T(8,128)} %get-tuple-element.276, s32[]{:T(128)} %get-tuple-element.263, pred[]{:T(512)S(6)} %compare.3, pred[]{:T(512)S(6)} %eq.67, pred[]{:T(512)S(6)} %lt.45, pred[]{:T(512)S(6)} %lt.46), kind=kLoop, calls=%fused_computation.clone.1 | loop fusion | flops 1310720 | bytes 3145736 | tf_op jit(solution)/shard_map/while/body/eval_jaxpr/jit(_where)/select_n | solution.py:20
  120.0 0.6 dynamic_slice.44
  121.9 1.8 %select_select_fusion.2 = f32[16,128,128]{2,1,0:T(8,128)S(1)} fusion(f32[16,128,128]{2,1,0:T(8,128)S(1)} %get-tuple-element.264, f32[8,16,128,128]{3,2,1,0:T(8,128)} %get-tuple-element.276, s32[]{:T(128)} %get-tuple-element.263, pred[]{:T(512)S(6)} %compare.3, pred[]{:T(512)S(6)} %eq.67, pred[]{:T(512)S(6)} %lt.45, pred[]{:T(512)S(6)} %lt.46), kind=kLoop, calls=%fused_computation.clone.1 | loop fusion | flops 1310720 | bytes 3145736 | tf_op jit(solution)/shard_map/while/body/eval_jaxpr/jit(_where)/select_n | solution.py:20
  124.3 0.6 dynamic_slice.44
  126.2 1.8 %select_select_fusion.2 = f32[16,128,128]{2,1,0:T(8,128)S(1)} fusion(f32[16,128,128]{2,1,0:T(8,128)S(1)} %get-tuple-element.264, f32[8,16,128,128]{3,2,1,0:T(8,128)} %get-tuple-element.276, s32[]{:T(128)} %get-tuple-element.263, pred[]{:T(512)S(6)} %compare.3, pred[]{:T(512)S(6)} %eq.67, pred[]{:T(512)S(6)} %lt.45, pred[]{:T(512)S(6)} %lt.46), kind=kLoop, calls=%fused_computation.clone.1 | loop fusion | flops 1310720 | bytes 3145736 | tf_op jit(solution)/shard_map/while/body/eval_jaxpr/jit(_where)/select_n | solution.py:20
  128.6 0.6 dynamic_slice.44
  130.5 1.8 %select_select_fusion.2 = f32[16,128,128]{2,1,0:T(8,128)S(1)} fusion(f32[16,128,128]{2,1,0:T(8,128)S(1)} %get-tuple-element.264, f32[8,16,128,128]{3,2,1,0:T(8,128)} %get-tuple-element.276, s32[]{:T(128)} %get-tuple-element.263, pred[]{:T(512)S(6)} %compare.3, pred[]{:T(512)S(6)} %eq.67, pred[]{:T(512)S(6)} %lt.45, pred[]{:T(512)S(6)} %lt.46), kind=kLoop, calls=%fused_computation.clone.1 | loop fusion | flops 1310720 | bytes 3145736 | tf_op jit(solution)/shard_map/while/body/eval_jaxpr/jit(_where)/select_n | solution.py:20
  132.9 5.1 %multiply_reduce_fusion = (f32[512]{0:T(512)S(1)}, f32[512,16,128]{0,2,1:T(8,128)}) fusion(f32[16,128,128]{2,1,0:T(8,128)S(1)} %get-tuple-element.182, pred[512]{0:T(512)(128)(4,1)S(1)} %broadcast_compare_fusion, f32[16,512,128]{1,2,0:T(8,128)} %fusion, bf16[512,2048]{1,0:T(8,128)(2,1)S(1)} %copy-done), kind=kOutput, calls=%fused_computation.5 | convolution fusion | flops 272891392 | bytes 11536896 | tf_op jit(solution)/shard_map/while/body/eval_jaxpr/thd,hde->the/dot_general | solution.py:73
  138.1 5.4 %copy.16 = f32[512,2048]{1,0:T(8,128)} copy(f32[512,2048]{0,1:T(8,128)} %bitcast.50) | data formatting | bytes 8388608 | tf_op jit(solution)/shard_map/reshape | solution.py:80
  143.4 9.9 %psum.7 = f32[512]{0:T(512)S(1)} all-reduce(f32[512]{0:T(512)S(1)} %get-tuple-element.216), channel_id=1, replica_groups=mesh['ctx'=8,'head'=4] {'head'}, use_global_device_ids=true, to_apply=%region_3.4 | all-reduce | flops 512 | bytes 4096 | tf_op jit(solution)/shard_map/psum | solution.py:82
  153.3 3.8 %multiply_convert_fusion = bf16[512,2048]{1,0:T(8,128)(2,1)} fusion(f32[512,2048]{1,0:T(8,128)} %copy.16, f32[512]{0:T(512)S(1)} %add_rsqrt_fusion), kind=kLoop, calls=%fused_computation.4 | loop fusion | flops 2097152 | bytes 6293504 | tf_op jit(solution)/shard_map/convert_element_type | solution.py:84
  (4 shorter events, 0.0 us)
Async XLA Ops:
  6.5 23.9 %copy-start = (bf16[512,2048]{1,0:T(8,128)(2,1)S(1)}, bf16[512,2048]{1,0:T(8,128)(2,1)}, u32[]{:S(2)}) copy-start(bf16[512,2048]{1,0:T(8,128)(2,1)} %param.6) | copy-start | bytes 6291460
  6.5 96.2 %all-gather.3.cloned.1.call-start = ((), (), s32[]{:S(2)}) async-start(), calls=%async_computation | async-start | bytes 9437184 | tf_op jit(solution)/shard_map/all_gather | solution.py:13
  13.7 4.6 %copy-start.2 = (u32[32]{0:T(128)S(1)}, u32[32]{0:T(128)}, u32[]{:S(2)}) copy-start(u32[32]{0:T(128)} %constant.91) | copy-start | bytes 388
  13.7 16.5 %copy-start.1 = (s32[512]{0:T(512)S(1)}, s32[512]{0:T(512)}, u32[]{:S(2)}) copy-start(s32[512]{0:T(512)} %param.9) | copy-start | bytes 6148
Sparse Core Ops, SparseCore 0:
  17.9 84.7 all-gather.2
where the time goes:
time: 165 us; the launch traced here: 164 us
  waiting for transfers between devices  62.9 us (38%)
  blocking collectives  20.5 us (12%)
  matrix products  18.5 us (11%)
  other arithmetic  17.5 us (11%)
  local copies, waits for them, and re-layouts  16.1 us (10%)
  between operations  14.6 us (9%)
  loops' own time  13.8 us (8%)
    all_gather x1, waiting for transfers between devices, carried_in(): pieces = jax.tree.map(lambda part: lax.all_gather(part, axis), value)  62.9 us
    another operation x1, loops' own time, carried_in(): return lax.fori_loop(0, count - 1, hop, running)  13.8 us
    select_n x7, other arithmetic, hop(): jnp.where(position < mine, new, old)  12.3 us
    unnamed x1, blocking collectives  10.6 us
    psum x1, blocking collectives, on_device(): totals = lax.psum(squares, 'head')  9.85 us
    dot_general x1, matrix products, local_block(): jnp.einsum('hts,shd->thd', probs, vb, preferred_element_type=jnp.float32)  9.32 us
    reshape x1, local copies, waits for them, and re-layouts, on_device(): outputs = (intra_all + inter_all).reshape(rows, heads * DH)  5.37 us
    dot_general x1, matrix products, inter_block(): jnp.einsum('thd,hde->the', qb, state.astype(jnp.bfloat16), preferred_elem...  5.13 us
  transfers between devices with their start and end apart: 1, of which 1 were waited for; matrix products, arithmetic and copies ran while one was open for 7% of the time, Pallas kernels for 0%

commit v1 on v0

v1 whole, which is shorter than its diff:
```python
import functools

import jax
import jax.numpy as jnp
from jax import lax
from jax.experimental import pallas as pl
from jax.experimental.pallas import tpu as pltpu
from jax.sharding import PartitionSpec as P

DH = 128
EPS = 1e-05
F32 = jnp.float32
BF16 = jnp.bfloat16
MESH = pl.DeviceIdType.MESH


def dot(a, b, dims):
    return lax.dot_general(a, b, (dims, ((), ())), preferred_element_type=F32)


def kernel(
    n_ctx, n_head,
    q_hbm, k_hbm, v_hbm, seg_ref, out_ref,
    q, k, v, o, mask, keep, seg_col, sq,
    kv_own, kv_send, kv_rcv, p_rcv, p_send, sb_own, sb_send, sb_rcv,
    tag_own, tag_partner, tag_odd, tag_prev, ss,
    in_sem, kv_ssem, kv_rsem, p_ssem, p_rsem, sb_ssem, sb_rsem, tag_ssem, tag_rsem, ss_ssem, ss_rsem,
):
    heads, rows, _ = q.shape
    hc = heads // 2
    half = rows // 2
    chips = n_ctx // 2
    ctx = lax.axis_index("ctx")
    me = lax.axis_index("head")
    core = ctx % 2
    chip = ctx // 2
    even = core == 0
    partner = ctx + 1 - 2 * core
    first, last = chip == 0, chip == chips - 1
    mine, other = core * hc, (1 - core) * hc

    def load(which, h):
        src, dst = ((k_hbm, k), (v_hbm, v), (q_hbm, q))[which]
        cols = pl.ds(pl.multiple_of(h * DH, DH), DH)
        return pltpu.make_async_copy(src.at[:, cols], dst.at[h], in_sem.at[which, h])

    def remote(src, dst, ssem, rsem, where):
        return pltpu.make_async_remote_copy(
            src_ref=src, dst_ref=dst, send_sem=ssem, recv_sem=rsem, device_id=where, device_id_type=MESH
        )

    def kv_copy(j):
        return remote(kv_send.at[j], kv_rcv.at[j], kv_ssem.at[j], kv_rsem.at[j], {"ctx": partner})

    def p_copy(j):
        return remote(p_send.at[j], p_rcv.at[j], p_ssem.at[j], p_rsem.at[j], {"ctx": ctx + 2})

    def sb_copy(j):
        return remote(sb_send.at[j], sb_rcv.at[j], sb_ssem.at[j], sb_rsem.at[j], {"ctx": partner})

    tag_pair = remote(tag_own, tag_partner, tag_ssem.at[0], tag_rsem.at[0], {"ctx": partner})
    tag_next = remote(tag_odd, tag_prev, tag_ssem.at[1], tag_rsem.at[1], {"ctx": ctx + 2})

    def ss_copy(d):
        return remote(ss.at[0], ss.at[d], ss_ssem.at[d], ss_rsem.at[d], {"head": lax.rem(me + d, n_head)})

    @pl.loop(0, hc)
    def _(j):
        for base in (other, mine):
            load(0, base + j).start()
            load(1, base + j).start()

    @pl.loop(0, heads)
    def _(h):
        load(2, h).start()

    barrier = pltpu.get_barrier_semaphore()
    pl.semaphore_signal(barrier, inc=1, device_id={"ctx": partner}, device_id_type=MESH)
    for d in range(1, n_head):
        pl.semaphore_signal(
            barrier, inc=1, device_id={"head": lax.rem(me + d, n_head)}, device_id_type=MESH
        )

    @pl.when(jnp.logical_not(first))
    def _():
        pl.semaphore_signal(barrier, inc=1, device_id={"ctx": ctx - 2}, device_id_type=MESH)

    @pl.when(jnp.logical_not(last))
    def _():
        pl.semaphore_signal(barrier, inc=1, device_id={"ctx": ctx + 2}, device_id_type=MESH)

    seg_row = seg_ref[...].astype(F32)
    seg_col[...] = jnp.broadcast_to(seg_row, (DH, rows)).T
    col = seg_col[...]
    tail = col[rows - 1:rows, :]
    tag_own[...] = jnp.broadcast_to(tail, tag_own.shape)
    keep[...] = jnp.where(col == tail, 1.0, 0.0).astype(BF16)
    t_at = lax.broadcasted_iota(jnp.int32, (rows, DH), 0)
    s_at = lax.broadcasted_iota(jnp.int32, (rows, DH), 1)
    for c in range(rows // DH):
        cut = slice(c * DH, (c + 1) * DH)
        seen = (col == seg_row[:, cut]) & (t_at >= s_at + c * DH)
        mask[:, cut] = jnp.where(seen, 1.0, 0.0).astype(BF16)
    sq[...] = jnp.zeros_like(sq)

    @pl.when(first)
    def _():
        p_rcv[...] = jnp.zeros_like(p_rcv)
        tag_prev[...] = jnp.full_like(tag_prev, -1.0)

    greeted = n_head + 2 - first.astype(jnp.int32) - last.astype(jnp.int32)
    pl.semaphore_wait(barrier, greeted)
    tag_pair.start()

    def state_of(h):
        load(0, h).wait()
        load(1, h).wait()
        return dot(k[h] * keep[...], v[h], ((0,), (0,)))

    def tag_even_row():
        return jnp.where(even, tag_own[0:1, :], tag_partner[0:1, :])

    def service(j):
        kv_copy(j).wait_recv()

        @pl.when(jnp.logical_not(first))
        def _():
            p_copy(j).wait_recv()

        own, got = kv_own[j], kv_rcv[j]
        kv_even = jnp.where(even, own, got)
        kv_odd = jnp.where(even, got, own)
        t_even = tag_even_row()
        stay_even = jnp.where(tag_prev[0:1, :] == t_even, 1.0, 0.0)
        stay_odd = jnp.where(t_even == tag_odd[0:1, :], 1.0, 0.0)
        before = p_rcv[j].astype(F32)
        middle = before * stay_even + kv_even

        @pl.when(jnp.logical_not(last))
        def _():
            p_send[j] = (middle * stay_odd + kv_odd).astype(p_send.dtype)
            p_copy(j).start()

        sb_own[j] = jnp.where(even, before, middle).astype(BF16)
        sb_send[j] = jnp.where(even, middle, before).astype(BF16)
        sb_copy(j).start()

    def kv_step(j):
        kv_send[j] = state_of(other + j)
        kv_copy(j).start()
        kv_own[j] = state_of(mine + j)

    kv_step(0)
    tag_pair.wait_recv()
    tag_odd[...] = jnp.where(even, tag_partner[...], tag_own[...])

    @pl.when(jnp.logical_not(last))
    def _():
        tag_next.start()

    @pl.loop(1, hc)
    def _(j):
        kv_step(j)

        @pl.when(first)
        def _():
            service(j - 1)

    @pl.when(first)
    def _():
        service(hc - 1)

    @pl.when(jnp.logical_not(first))
    def _():
        tag_next.wait_recv()

    lag = heads // 4

    @pl.loop(0, heads)
    def _(h):
        load(2, h).wait()
        low = dot(q[h, :half, :], k[h, :half, :], ((1,), (1,))).astype(BF16) * mask[:half, :half]
        high = dot(q[h, half:, :], k[h], ((1,), (1,))).astype(BF16) * mask[half:, :]
        o[h, :half, :] = dot(low, v[h, :half, :], ((1,), (0,)))
        o[h, half:, :] = dot(high, v[h], ((1,), (0,)))
        turn = h - lag * chip

        @pl.when(jnp.logical_not(first) & jnp.logical_not(last) & (turn >= 0) & (turn < hc))
        def _():
            service(turn)

    t_last = jnp.where(even, tag_prev[0:1, :], tag_even_row())
    keep[...] = jnp.where(seg_col[...] == t_last, 1.0, 0.0).astype(BF16)

    def add_inter(h, state):
        total = o[h] + dot(q[h] * keep[...], state, ((1,), (0,)))
        o[h] = total
        sq[...] += total * total

    def finish_other(j):
        sb_copy(j).wait_recv()
        add_inter(other + j, sb_rcv[j])

    @pl.loop(0, hc)
    def _(j):
        @pl.when(jnp.logical_not(first) & (last | (lag * chip + j >= heads)))
        def _():
            service(j)

        @pl.when(j > 0)
        def _():
            finish_other(j - 1)

        add_inter(mine + j, sb_own[j])

    finish_other(hc - 1)

    spread = sq[...].T
    ss[0] = jnp.sum(spread.reshape(DH // 8, 8, rows), axis=0)
    for d in range(1, n_head):
        ss_copy(d).start()
    total = ss[0]
    for d in range(1, n_head):
        ss_copy(d).wait_recv()
        total = total + ss[d]
    mean = jnp.sum(total, axis=0, keepdims=True) / (heads * n_head * DH)
    sq[...] = jnp.broadcast_to(lax.rsqrt(mean + EPS), (DH, rows)).T

    for h in range(heads):
        out_ref[:, h * DH:(h + 1) * DH] = (o[h] * sq[...]).astype(BF16)

    tag_pair.wait_send()
    for d in range(1, n_head):
        ss_copy(d).wait_send()

    @pl.when(jnp.logical_not(last))
    def _():
        tag_next.wait_send()

    @pl.loop(0, hc)
    def _(j):
        kv_copy(j).wait_send()
        sb_copy(j).wait_send()

        @pl.when(jnp.logical_not(last))
        def _():
            p_copy(j).wait_send()


def on_device(n_ctx, n_head, queries, keys, values, segment_ids):
    rows, cols = queries.shape
    heads = cols // DH
    hc = heads // 2
    wire = BF16 if n_ctx <= 16 else F32
    vmem, dma = pltpu.VMEM, pltpu.SemaphoreType.DMA
    big = vmem((heads, rows, DH), BF16)
    state = vmem((hc, DH, DH), F32)
    state_p = vmem((hc, DH, DH), wire)
    state_b = vmem((hc, DH, DH), BF16)
    tag = vmem((8, DH), F32)
    anywhere = pl.BlockSpec(memory_space=pl.ANY)
    inside = pl.BlockSpec(memory_space=pltpu.VMEM)
    return pl.pallas_call(
        functools.partial(kernel, n_ctx, n_head),
        out_shape=jax.ShapeDtypeStruct((rows, cols), BF16),
        in_specs=[anywhere, anywhere, anywhere, inside],
        out_specs=inside,
        scratch_shapes=[
            big, big, big,
            vmem((heads, rows, DH), F32),
            vmem((rows, rows), BF16),
            vmem((rows, DH), BF16),
            vmem((rows, DH), F32),
            vmem((rows, DH), F32),
            state, state, state, state_p, state_p, state_b, state_b, state_b,
            tag, tag, tag, tag,
            vmem((n_head, 8, rows), F32),
            dma((3, heads)),
            dma((hc,)), dma((hc,)), dma((hc,)), dma((hc,)), dma((hc,)), dma((hc,)),
            dma((2,)), dma((2,)), dma((n_head,)), dma((n_head,)),
        ],
        compiler_params=pltpu.CompilerParams(
            collective_id=0, has_side_effects=True, vmem_limit_bytes=48 * 2**20
        ),
        cost_estimate=pl.CostEstimate(
            flops=2 * heads * rows * DH * (2 * rows + 2 * DH), bytes_accessed=8 * rows * cols, transcendentals=rows
        ),
    )(queries, keys, values, segment_ids.reshape(1, rows))


def solution(mesh):
    n_ctx, n_head = mesh.shape["ctx"], mesh.shape["head"]
    in_specs = (P("ctx", "head"), P("ctx", "head"), P("ctx", "head"), P("ctx"))
    return jax.shard_map(
        functools.partial(on_device, n_ctx, n_head),
        mesh=mesh, in_specs=in_specs, out_specs=P("ctx", "head"), check_vma=False,
    )
```

time: 165 us -> 29.1 us (0.18)
  the two profiles are of different devices: /device:TPU:0 before, /device:TPU:24 now
where the time goes in v1:
time: 29.1 us; the launch traced here: 29 us
  Pallas kernels  25.4 us (87%)
  local copies, waits for them, and re-layouts  3.59 us (12%)
    pallas_call x1, Pallas kernels, on_device(): pl.pallas_call(functools.partial(kernel, n_ctx, n_head), out_shape=jax.Sh...  25.4 us
    unnamed x5, local copies, waits for them, and re-layouts  3.59 us

profile of v1, /device:TPU:24, one launch (start us, length us, event | category | flops | bytes accessed | tf_op | source)
XLA Modules:
  0.0 29.0 jit_solution(17252852062146266484)
XLA Ops:
  0.0 0.0 copy-start
  0.0 1.6 %copy-done = bf16[512,2048]{1,0:T(8,128)(2,1)S(1)} copy-done((bf16[512,2048]{1,0:T(8,128)(2,1)S(1)}, bf16[512,2048]{1,0:T(8,128)(2,1)}, u32[]{:S(2)}) %copy-start) | copy-done | bytes 2097176
  1.6 0.0 copy-start.1
  1.6 0.7 %copy-done.1 = s32[512]{0:T(512)S(1)} copy-done((s32[512]{0:T(512)S(1)}, s32[512]{0:T(512)}, u32[]{:S(2)}) %copy-start.1) | copy-done | bytes 2072
  2.3 25.4 %shard_map.46 = bf16[512,2048]{1,0:T(8,128)(2,1)S(1)} custom-call(bf16[512,2048]{1,0:T(8,128)(2,1)S(1)} %copy-done, bf16[512,2048]{1,0:T(8,128)(2,1)} %k_hbm.1, bf16[512,2048]{1,0:T(8,128)(2,1)} %v_hbm.1, s32[1,512]{1,0:T(1,128)S(1)} %bitcast.1), custom_call_target="tpu_custom_call" | custom-call | flops 2684354560 | bytes 8388608 | tf_op jit(solution)/shard_map/pallas_call | solution.py:263
  27.6 1.3 %copy.6 = bf16[512,2048]{1,0:T(8,128)(2,1)} copy(bf16[512,2048]{1,0:T(8,128)(2,1)S(1)} %shard_map.46) | data formatting | bytes 4194304
Async XLA Ops:
  0.0 1.6 %copy-start = (bf16[512,2048]{1,0:T(8,128)(2,1)S(1)}, bf16[512,2048]{1,0:T(8,128)(2,1)}, u32[]{:S(2)}) copy-start(bf16[512,2048]{1,0:T(8,128)(2,1)} %q_hbm.1) | copy-start | bytes 6291460
  1.6 0.7 %copy-start.1 = (s32[512]{0:T(512)S(1)}, s32[512]{0:T(512)}, u32[]{:S(2)}) copy-start(s32[512]{0:T(512)} %param.7) | copy-start | bytes 6148

commit v2 on v1

--- a/solution.py
+++ b/solution.py
@@ -20,11 +20,11 @@
 
 def kernel(
     n_ctx, n_head,
-    q_hbm, k_hbm, v_hbm, seg_ref, out_ref,
-    q, k, v, o, mask, keep, seg_col, sq,
+    q_hbm, k_hbm, v_hbm, seg_hbm, out_ref,
+    q, k, v, seg, o, mask, keep, seg_col, sq,
     kv_own, kv_send, kv_rcv, p_rcv, p_send, sb_own, sb_send, sb_rcv,
     tag_own, tag_partner, tag_odd, tag_prev, ss,
-    in_sem, kv_ssem, kv_rsem, p_ssem, p_rsem, sb_ssem, sb_rsem, tag_ssem, tag_rsem, ss_ssem, ss_rsem,
+    in_sem, seg_sem, kv_ssem, kv_rsem, p_ssem, p_rsem, sb_ssem, sb_rsem, tag_ssem, tag_rsem, ss_ssem, ss_rsem,
 ):
     heads, rows, _ = q.shape
     hc = heads // 2
@@ -64,6 +64,9 @@
     def ss_copy(d):
         return remote(ss.at[0], ss.at[d], ss_ssem.at[d], ss_rsem.at[d], {"head": lax.rem(me + d, n_head)})
 
+    seg_load = pltpu.make_async_copy(seg_hbm, seg, seg_sem)
+    seg_load.start()
+
     @pl.loop(0, hc)
     def _(j):
         for base in (other, mine):
@@ -89,7 +92,8 @@
     def _():
         pl.semaphore_signal(barrier, inc=1, device_id={"ctx": ctx + 2}, device_id_type=MESH)
 
-    seg_row = seg_ref[...].astype(F32)
+    seg_load.wait()
+    seg_row = seg[...].astype(F32)
     seg_col[...] = jnp.broadcast_to(seg_row, (DH, rows)).T
     col = seg_col[...]
     tail = col[rows - 1:rows, :]
@@ -112,11 +116,6 @@
     pl.semaphore_wait(barrier, greeted)
     tag_pair.start()
 
-    def state_of(h):
-        load(0, h).wait()
-        load(1, h).wait()
-        return dot(k[h] * keep[...], v[h], ((0,), (0,)))
-
     def tag_even_row():
         return jnp.where(even, tag_own[0:1, :], tag_partner[0:1, :])
 
@@ -146,9 +145,17 @@
         sb_copy(j).start()
 
     def kv_step(j):
-        kv_send[j] = state_of(other + j)
-        kv_copy(j).start()
-        kv_own[j] = state_of(mine + j)
+        ahead = [(base + j + i) for i in range(2) for base in (other, mine)]
+        for h in ahead:
+            load(0, h).wait()
+            load(1, h).wait()
+        stay = keep[...]
+        sums = [dot(k[h] * stay, v[h], ((0,), (0,))) for h in ahead]
+        for i in range(2):
+            kv_send[j + i] = sums[2 * i]
+            kv_own[j + i] = sums[2 * i + 1]
+        for i in range(2):
+            kv_copy(j + i).start()
 
     kv_step(0)
     tag_pair.wait_recv()
@@ -158,62 +165,79 @@
     def _():
         tag_next.start()
 
-    @pl.loop(1, hc)
+    @pl.loop(2, hc, step=2)
     def _(j):
         kv_step(j)
 
         @pl.when(first)
         def _():
+            service(j - 2)
             service(j - 1)
 
     @pl.when(first)
     def _():
+        service(hc - 2)
         service(hc - 1)
 
     @pl.when(jnp.logical_not(first))
     def _():
         tag_next.wait_recv()
 
-    lag = heads // 4
-
-    @pl.loop(0, heads)
+    lag = max(2, heads // 4 // 2 * 2)
+
+    @pl.loop(0, heads, step=2)
     def _(h):
-        load(2, h).wait()
-        low = dot(q[h, :half, :], k[h, :half, :], ((1,), (1,))).astype(BF16) * mask[:half, :half]
-        high = dot(q[h, half:, :], k[h], ((1,), (1,))).astype(BF16) * mask[half:, :]
-        o[h, :half, :] = dot(low, v[h, :half, :], ((1,), (0,)))
-        o[h, half:, :] = dot(high, v[h], ((1,), (0,)))
+        for i in range(2):
+            load(2, h + i).wait()
+        tops = [dot(q[h + i, :half, :], k[h + i, :half, :], ((1,), (1,))) for i in range(2)]
+        ends = [dot(q[h + i, half:, :], k[h + i], ((1,), (1,))) for i in range(2)]
+        tops = [part.astype(BF16) * mask[:half, :half] for part in tops]
+        ends = [part.astype(BF16) * mask[half:, :] for part in ends]
+        for i in range(2):
+            o[h + i, :half, :] = dot(tops[i], v[h + i, :half, :], ((1,), (0,)))
+            o[h + i, half:, :] = dot(ends[i], v[h + i], ((1,), (0,)))
         turn = h - lag * chip
 
         @pl.when(jnp.logical_not(first) & jnp.logical_not(last) & (turn >= 0) & (turn < hc))
         def _():
             service(turn)
+            service(turn + 1)
 
     t_last = jnp.where(even, tag_prev[0:1, :], tag_even_row())
     keep[...] = jnp.where(seg_col[...] == t_last, 1.0, 0.0).astype(BF16)
 
-    def add_inter(h, state):
-        total = o[h] + dot(q[h] * keep[...], state, ((1,), (0,)))
-        o[h] = total
-        sq[...] += total * total
-
-    def finish_other(j):
-        sb_copy(j).wait_recv()
-        add_inter(other + j, sb_rcv[j])
-
-    @pl.loop(0, hc)
+    def add_inter(pieces):
+        here = keep[...]
+        squares = sq[...]
+        for h, state in pieces:
+            total = o[h] + dot(q[h] * here, state[...], ((1,), (0,)))
+            o[h] = total
+            squares = squares + total * total
+        sq[...] = squares
+
+    def late_service(j):
+        @pl.when(jnp.logical_not(first) & (last | (lag * chip + j >= heads)))
+        def _():
+            service(j)
+            service(j + 1)
+
+    def own_pieces(j):
+        return [(mine + j + i, sb_own.at[j + i]) for i in range(2)]
+
+    def other_pieces(j):
+        for i in range(2):
+            sb_copy(j + i).wait_recv()
+        return [(other + j + i, sb_rcv.at[j + i]) for i in range(2)]
+
+    late_service(0)
+    add_inter(own_pieces(0))
+
+    @pl.loop(2, hc, step=2)
     def _(j):
-        @pl.when(jnp.logical_not(first) & (last | (lag * chip + j >= heads)))
-        def _():
-            service(j)
-
-        @pl.when(j > 0)
-        def _():
-            finish_other(j - 1)
-
-        add_inter(mine + j, sb_own[j])
-
-    finish_other(hc - 1)
+        late_service(j)
+        add_inter(other_pieces(j - 2) + own_pieces(j))
+
+    add_inter(other_pieces(hc - 2))
 
     spread = sq[...].T
     ss[0] = jnp.sum(spread.reshape(DH // 8, 8, rows), axis=0)
@@ -262,11 +286,12 @@
     inside = pl.BlockSpec(memory_space=pltpu.VMEM)
     return pl.pallas_call(
         functools.partial(kernel, n_ctx, n_head),
-        out_shape=jax.ShapeDtypeStruct((rows, cols), BF16),
-        in_specs=[anywhere, anywhere, anywhere, inside],
+        out_shape=pltpu.VMEM((rows, cols), BF16),
+        in_specs=[anywhere, anywhere, anywhere, anywhere],
         out_specs=inside,
         scratch_shapes=[
             big, big, big,
+            vmem((1, rows), jnp.int32),
             vmem((heads, rows, DH), F32),
             vmem((rows, rows), BF16),
             vmem((rows, DH), BF16),
@@ -275,12 +300,12 @@
             state, state, state, state_p, state_p, state_b, state_b, state_b,
             tag, tag, tag, tag,
             vmem((n_head, 8, rows), F32),
-            dma((3, heads)),
+            dma((3, heads)), dma,
             dma((hc,)), dma((hc,)), dma((hc,)), dma((hc,)), dma((hc,)), dma((hc,)),
             dma((2,)), dma((2,)), dma((n_head,)), dma((n_head,)),
         ],
         compiler_params=pltpu.CompilerParams(
-            collective_id=0, has_side_effects=True, vmem_limit_bytes=48 * 2**20
+            collective_id=0, has_side_effects=True, vmem_limit_bytes=60 * 2**20
         ),
         cost_estimate=pl.CostEstimate(
             flops=2 * heads * rows * DH * (2 * rows + 2 * DH), bytes_accessed=8 * rows * cols, transcendentals=rows

time: 29.1 us -> 23.6 us (0.81)
  the two profiles are of different devices: /device:TPU:24 before, /device:TPU:25 now
where the time goes in v2:
time: 23.6 us; the launch traced here: 23.4 us
  Pallas kernels  22.1 us (94%)
  local copies, waits for them, and re-layouts  1.32 us (6%)
    pallas_call x1, Pallas kernels, on_device(): pl.pallas_call(functools.partial(kernel, n_ctx, n_head), out_shape=pltpu....  22.1 us
    unnamed x1, local copies, waits for them, and re-layouts  1.32 us

profile of v2, /device:TPU:25, one launch (start us, length us, event | category | flops | bytes accessed | tf_op | source)
XLA Modules:
  0.0 23.4 jit_solution(12069937773162961809)
XLA Ops:
  0.0 22.1 %shard_map.46 = bf16[512,2048]{1,0:T(8,128)(2,1)S(1)} custom-call(bf16[512,2048]{1,0:T(8,128)(2,1)} %q_hbm.1, bf16[512,2048]{1,0:T(8,128)(2,1)} %k_hbm.1, bf16[512,2048]{1,0:T(8,128)(2,1)} %v_hbm.1, s32[1,512]{1,0:T(1,128)} %bitcast.1), custom_call_target="tpu_custom_call" | custom-call | flops 2684354560 | bytes 8388608 | tf_op jit(solution)/shard_map/pallas_call | solution.py:287
  22.1 1.3 %copy.6 = bf16[512,2048]{1,0:T(8,128)(2,1)} copy(bf16[512,2048]{1,0:T(8,128)(2,1)S(1)} %shard_map.46) | data formatting | bytes 4194304

commit v3 on v2

--- a/solution.py
+++ b/solution.py
@@ -73,10 +73,6 @@
             load(0, base + j).start()
             load(1, base + j).start()
 
-    @pl.loop(0, heads)
-    def _(h):
-        load(2, h).start()
-
     barrier = pltpu.get_barrier_semaphore()
     pl.semaphore_signal(barrier, inc=1, device_id={"ctx": partner}, device_id_type=MESH)
     for d in range(1, n_head):
@@ -99,12 +95,6 @@
     tail = col[rows - 1:rows, :]
     tag_own[...] = jnp.broadcast_to(tail, tag_own.shape)
     keep[...] = jnp.where(col == tail, 1.0, 0.0).astype(BF16)
-    t_at = lax.broadcasted_iota(jnp.int32, (rows, DH), 0)
-    s_at = lax.broadcasted_iota(jnp.int32, (rows, DH), 1)
-    for c in range(rows // DH):
-        cut = slice(c * DH, (c + 1) * DH)
-        seen = (col == seg_row[:, cut]) & (t_at >= s_at + c * DH)
-        mask[:, cut] = jnp.where(seen, 1.0, 0.0).astype(BF16)
     sq[...] = jnp.zeros_like(sq)
 
     @pl.when(first)
@@ -157,6 +147,10 @@
         for i in range(2):
             kv_copy(j + i).start()
 
+    @pl.loop(0, heads)
+    def _(h):
+        load(2, h).start()
+
     kv_step(0)
     tag_pair.wait_recv()
     tag_odd[...] = jnp.where(even, tag_partner[...], tag_own[...])
@@ -183,7 +177,15 @@
     def _():
         tag_next.wait_recv()
 
-    lag = max(2, heads // 4 // 2 * 2)
+    col = seg_col[...]
+    seg_row = seg[...].astype(F32)
+    t_at = lax.broadcasted_iota(jnp.int32, (rows, DH), 0)
+    s_at = lax.broadcasted_iota(jnp.int32, (rows, DH), 1)
+    for c in range(rows // DH):
+        cut = slice(c * DH, (c + 1) * DH)
+        seen = (col == seg_row[:, cut]) & (t_at >= s_at + c * DH)
+        mask[:, cut] = jnp.where(seen, 1.0, 0.0).astype(BF16)
+    begin = 2 * chip
 
     @pl.loop(0, heads, step=2)
     def _(h):
@@ -196,7 +198,7 @@
         for i in range(2):
             o[h + i, :half, :] = dot(tops[i], v[h + i, :half, :], ((1,), (0,)))
             o[h + i, half:, :] = dot(ends[i], v[h + i], ((1,), (0,)))
-        turn = h - lag * chip
+        turn = h - begin
 
         @pl.when(jnp.logical_not(first) & jnp.logical_not(last) & (turn >= 0) & (turn < hc))
         def _():
@@ -216,7 +218,7 @@
         sq[...] = squares
 
     def late_service(j):
-        @pl.when(jnp.logical_not(first) & (last | (lag * chip + j >= heads)))
+        @pl.when(jnp.logical_not(first) & (last | (begin + j >= heads)))
         def _():
             service(j)
             service(j + 1)
@@ -250,8 +252,10 @@
     mean = jnp.sum(total, axis=0, keepdims=True) / (heads * n_head * DH)
     sq[...] = jnp.broadcast_to(lax.rsqrt(mean + EPS), (DH, rows)).T
 
-    for h in range(heads):
-        out_ref[:, h * DH:(h + 1) * DH] = (o[h] * sq[...]).astype(BF16)
+    for r in range(0, rows, 64):
+        scale = sq[r:r + 64, :]
+        for h in range(heads):
+            out_ref[r:r + 64, h * DH:(h + 1) * DH] = (o[h, r:r + 64, :] * scale).astype(BF16)
 
     tag_pair.wait_send()
     for d in range(1, n_head):

time: 23.6 us -> 22.9 us (0.970)
  Pallas kernels: 22.1 us -> 21.4 us
    pallas_call x1, Pallas kernels: 22.1 us -> 21.4 us  [on_device(): pl.pallas_call(functools.partial(kernel, n_ctx, n_head), out_shape=pltpu....]
where the time goes in v3:
time: 22.9 us; the launch traced here: 22.8 us
  Pallas kernels  21.4 us (93%)
  local copies, waits for them, and re-layouts  1.32 us (6%)
    pallas_call x1, Pallas kernels, on_device(): pl.pallas_call(functools.partial(kernel, n_ctx, n_head), out_shape=pltpu....  21.4 us
    unnamed x1, local copies, waits for them, and re-layouts  1.32 us

profile of v3, /device:TPU:25, one launch (start us, length us, event | category | flops | bytes accessed | tf_op | source)
XLA Modules:
  0.0 22.8 jit_solution(7802150737951067671)
XLA Ops:
  0.0 21.4 %shard_map.46 = bf16[512,2048]{1,0:T(8,128)(2,1)S(1)} custom-call(bf16[512,2048]{1,0:T(8,128)(2,1)} %q_hbm.1, bf16[512,2048]{1,0:T(8,128)(2,1)} %k_hbm.1, bf16[512,2048]{1,0:T(8,128)(2,1)} %v_hbm.1, s32[1,512]{1,0:T(1,128)} %bitcast.1), custom_call_target="tpu_custom_call" | custom-call | flops 2684354560 | bytes 8388608 | tf_op jit(solution)/shard_map/pallas_call | solution.py:291
  21.4 1.3 %copy.6 = bf16[512,2048]{1,0:T(8,128)(2,1)} copy(bf16[512,2048]{1,0:T(8,128)(2,1)S(1)} %shard_map.46) | data formatting | bytes 4194304
